TPU v7x, 32 devices: a whole 2x2x4 slice. The times are simulated.
32 devices in a mesh: grp: 8 (over y, x, core), loc: 4 (over z).
Axes of the slice: x: 2, y: 2, z: 4, core: 2. Of those that a mesh axis runs over, the one named last changes fastest.
Arguments:
- tokens: bfloat16 [4096, 2048], P(('grp', 'loc')), may hold values from -6 to 6
- norm_gain: bfloat16 [2048], replicated, may hold values from 0.099609375 to 1.8984375
- w_gate: bfloat16 [32, 2048, 384], P(('grp', 'loc')), may hold values from -0.125 to 0.125
- w_up: bfloat16 [32, 2048, 384], P(('grp', 'loc')), may hold values from -0.125 to 0.125
- w_down: bfloat16 [32, 384, 2048], P(('grp', 'loc')), may hold values from -0.21875 to 0.21875
- expert_ids: int32 [4096, 8], P(('grp', 'loc')), may hold values from 0 to 15, as said below
- gate_num: int32 [4096, 8], P(('grp', 'loc')), may hold values from 32 to 255
Outputs:
- mixed: bfloat16 [4096, 2048], P(('grp', 'loc'))
Inputs may be any that keep to these rules, and one draw needn't show every extreme that they name: `expert_ids`: each token names 4 different groups (group of expert e: e // 2) and two different experts in each, listed group after group in increasing order. Of the 128 tokens of one device at most 128 use any one group, and every device has a group used by exactly 128 of its tokens. The tokens of all devices with one loc index use each group exactly 512 times in all, and each expert of that group exactly 512 times.
All inputs are finite; a program needn't handle non-finite values.
Results may differ from a plain program's by a relative error of at most 0.0038.
Values may be sent and summed in bfloat16 or wider, within the bound.
A program may use at most 128 MiB of HBM per device.

v0:
```python
import jax
import jax.numpy as jnp
from jax import lax
from jax.sharding import PartitionSpec as P

GTOP = 4


epsilon = 1e-06
denominator = 1024.0


def from_partner(value, axis, apart):
    mask = 2**apart
    pairs = [(source, source ^ mask) for source in range(lax.axis_size(axis))]
    return lax.ppermute(value, axis, pairs)


def ordered_pair(own_part, other_part, is_lower, axis_index):
    lower_part = jnp.where(is_lower, own_part, other_part)
    upper_part = jnp.where(is_lower, other_part, own_part)
    return jnp.concatenate([lower_part, upper_part], axis=axis_index)


def shards(tokens, norm_gain, w_gate, w_up, w_down, expert_ids, gate_num):
    group_count = lax.axis_size("grp")
    local_count = lax.axis_size("loc")
    rows_dev, model_width = tokens.shape
    top_count = expert_ids.shape[1]
    experts_group = local_count // 2
    capacity = 2 * rows_dev * GTOP // group_count
    expert_rows = rows_dev * GTOP * (top_count // GTOP) // experts_group
    half_rows = expert_rows // 2
    slots_all = group_count * capacity
    inputs_float = tokens.astype(jnp.float32)
    inv_scale = lax.rsqrt(jnp.mean(inputs_float * inputs_float, axis=-1, keepdims=True) + epsilon)
    normed = (inputs_float * inv_scale * norm_gain.astype(jnp.float32)).astype(jnp.bfloat16)
    owner_group = expert_ids // experts_group
    group_range = jnp.arange(group_count, dtype=jnp.int32)
    member = jnp.any(owner_group[:, :, None] == group_range[None, None, :], axis=1)
    position = jnp.cumsum(member.astype(jnp.int32), axis=0) - 1
    slot_range = jnp.arange(capacity, dtype=jnp.int32)
    slot_table = member.T[:, None, :] & (position.T[:, None, :] == slot_range[None, :, None])
    dispatch_matrix = slot_table.reshape(slots_all, rows_dev).astype(jnp.bfloat16)
    packed = jnp.dot(dispatch_matrix, normed, preferred_element_type=jnp.float32).astype(
        jnp.bfloat16
    )
    packed = packed.reshape(group_count, capacity, model_width)
    filled = jnp.any(slot_table, axis=2).reshape(slots_all)
    token_range = jnp.arange(rows_dev, dtype=jnp.int32)
    source_token = jnp.sum(
        slot_table.astype(jnp.int32) * token_range[None, None, :], axis=2
    ).reshape(slots_all)
    details = jnp.concatenate([expert_ids, gate_num], axis=1)[source_token]
    details = jnp.where(filled[:, None], details, -1).astype(jnp.bfloat16)
    details = details.reshape(group_count, capacity, 2 * top_count)
    arrived, arrived_details = (
        lax.all_to_all(packed, "grp", split_axis=0, concat_axis=0, tiled=True),
        lax.all_to_all(details, "grp", split_axis=0, concat_axis=0, tiled=True),
    )
    arrived = arrived.reshape(slots_all, model_width)
    arrived_details = arrived_details.reshape(slots_all, 2 * top_count).astype(jnp.int32)
    own_group = lax.axis_index("grp")
    own_half = lax.axis_index("loc") % 2
    is_lower = own_half == 0
    arrived_ids = arrived_details[:, :top_count]
    arrived_nums = arrived_details[:, top_count:]
    local_ids = arrived_ids - own_group * experts_group
    inside = (arrived_ids >= 0) & (local_ids >= 0) & (local_ids < experts_group)
    expert_range = jnp.arange(experts_group, dtype=jnp.int32)
    chosen = jnp.any(
        inside[:, :, None] & (local_ids[:, :, None] == expert_range[None, None, :]), axis=1
    )
    ranking = jnp.cumsum(chosen.astype(jnp.int32), axis=0) - 1
    slot_index = jnp.broadcast_to(jnp.arange(slots_all, dtype=jnp.int32)[:, None], chosen.shape)
    base_index = 2 * expert_range[None, :] * expert_rows + ranking
    spill_index = local_count * expert_rows
    target_lower = jnp.where(chosen, base_index, spill_index)
    target_upper = jnp.where(chosen, base_index + expert_rows, spill_index)
    source_slot = jnp.zeros((spill_index,), jnp.int32)
    source_slot = source_slot.at[target_lower.reshape(-1)].set(slot_index.reshape(-1), mode="drop")
    source_slot = source_slot.at[target_upper.reshape(-1)].set(slot_index.reshape(-1), mode="drop")
    outgoing = arrived[source_slot].reshape(local_count, expert_rows, model_width)
    received = lax.all_to_all(outgoing, "loc", split_axis=0, concat_axis=0, tiled=True)
    flat_rows = received.reshape(-1, model_width)
    gate_act = jnp.dot(flat_rows, w_gate[0], preferred_element_type=jnp.float32)
    up_act = jnp.dot(flat_rows, w_up[0], preferred_element_type=jnp.float32)
    hidden = (jax.nn.silu(gate_act) * up_act).astype(jnp.bfloat16)
    hidden = hidden.reshape(local_count, expert_rows, w_gate.shape[2])
    own_hidden = lax.dynamic_slice_in_dim(hidden, own_half * half_rows, half_rows, 1)
    given_hidden = lax.dynamic_slice_in_dim(hidden, (1 - own_half) * half_rows, half_rows, 1)
    taken_hidden, other_down = from_partner((given_hidden, w_down[0]), "loc", 0)
    hidden_full = ordered_pair(own_hidden, taken_hidden, is_lower, 2)
    down_full = ordered_pair(w_down[0], other_down, is_lower, 0)
    result = jnp.dot(
        hidden_full.reshape(-1, hidden_full.shape[2]), down_full, preferred_element_type=jnp.float32
    )
    result = result.astype(jnp.bfloat16).reshape(local_count, half_rows, model_width)
    returned = lax.all_to_all(result, "loc", split_axis=0, concat_axis=0, tiled=True)
    flat_returned = returned.reshape(-1, model_width)
    filled_slot = jnp.any(inside, axis=1)
    first_pick = jnp.argmax(inside, axis=1)
    second_pick = top_count - 1 - jnp.argmax(inside[:, ::-1], axis=1)

    def pick_term(which):
        local_pick = jnp.take_along_axis(local_ids, which[:, None], axis=1)[:, 0]
        local_pick = jnp.where(filled_slot, local_pick, 0)
        rank_pick = jnp.take_along_axis(ranking, local_pick[:, None], axis=1)[:, 0]
        row_pick = (2 * local_pick + rank_pick // half_rows) * half_rows + rank_pick % half_rows
        row_pick = jnp.where(filled_slot, row_pick, 0)
        weight = jnp.take_along_axis(arrived_nums, which[:, None], axis=1)[:, 0]
        weight = jnp.where(filled_slot, weight, 0).astype(jnp.float32) / denominator
        return weight[:, None] * flat_returned[row_pick].astype(jnp.float32)

    group_sum = (pick_term(first_pick) + pick_term(second_pick)).astype(jnp.bfloat16)
    group_sum = group_sum.reshape(group_count, capacity, model_width)
    returned_sums = lax.all_to_all(group_sum, "grp", split_axis=0, concat_axis=0, tiled=True)
    mixed_sum = jnp.dot(
        dispatch_matrix.T,
        returned_sums.reshape(slots_all, model_width),
        preferred_element_type=jnp.float32,
    )
    return (inputs_float + mixed_sum).astype(jnp.bfloat16)


def solution(mesh):
    return jax.shard_map(
        shards,
        mesh=mesh,
        in_specs=(
            P(("grp", "loc"), None),
            P(),
            P(("grp", "loc"), None, None),
            P(("grp", "loc"), None, None),
            P(("grp", "loc"), None, None),
            P(("grp", "loc"), None),
            P(("grp", "loc"), None),
        ),
        out_specs=P(("grp", "loc"), None),
        check_vma=False,
    )
```

profile of v0, /device:TPU:0, one launch (start us, length us, event | category | flops | bytes accessed | tf_op | source)
XLA Modules:
  0.0 496.7 jit_solution(1270753796932786307)
XLA Ops:
  0.0 0.9 copy.71
  1.0 0.0 copy-start.4
  1.0 0.0 copy-start.2
  1.1 0.1 copy.76
  1.2 0.2 reduce_window_sum.24
  1.4 0.2 select_reduce_fusion
  1.6 0.2 fusion.18
  1.9 0.7 pad_add_fusion.4
  2.6 0.1 copy.78
  2.7 2.8 gather_fusion
  5.5 0.2 copy.79
  5.7 0.6 select_convert_fusion
  6.3 5.2 %all-to-all-start = ((bf16[8,128,16]{1,2,0:T(8,128)(2,1)}), bf16[8,128,16]{1,2,0:T(8,128)(2,1)S(1)}, u32[]{:S(2)}, u32[]{:S(2)}) async-start(bf16[8,128,16]{1,2,0:T(8,128)(2,1)} %select_convert_fusion), calls=%async_computation | async-start | bytes 65536 | tf_op jit(solution)/shard_map/all_to_all | solution.py:59
  11.5 0.2 fusion.19
  11.7 0.2 fusion.10
  11.9 3.3 convolution_convert_fusion.1
  15.2 1.1 all-to-all-done
  16.3 4.6 all-to-all-start.1
  21.0 0.3 reshape.340
  21.4 0.6 reduce-window.6
  22.0 0.2 slice_reduce_fusion
  22.2 0.2 reduce-window.9
  22.4 0.1 add_bitcast_fusion.1
  22.4 0.1 add_select_fusion.1
  22.5 0.2 copy.81
  22.7 0.3 reshape.231
  23.1 0.2 copy.82
  23.3 0.3 reshape.233
  23.6 8.0 %scatter_custom_fusion = s32[2048]{0:T(1024)S(1)} fusion(s32[2048]{0:T(1024)S(1)} %bitcast.156, s32[2048]{0:T(1024)S(1)} %reshape.340, s32[]{:T(128)} %constant.128.clone.1), kind=kCustom, calls=%fused_computation.141 | custom fusion | bytes 8196 | tf_op jit(solution)/shard_map/scatter | solution.py:81
  31.7 8.1 %scatter_fusion = s32[2048]{0:T(1024)S(1)} fusion(s32[2048]{0:T(1024)S(1)} %scatter_custom_fusion, s32[2048]{0:T(1024)S(1)} %bitcast.144, s32[2048]{0:T(1024)S(1)} %reshape.340), kind=kCustom, calls=%fused_computation.11 | custom fusion | bytes 32768 | tf_op jit(solution)/shard_map/scatter | solution.py:82
  39.8 30.3 %all-to-all-done.1 = bf16[8,128,2048]{2,1,0:T(8,128)(2,1)} async-done(((bf16[8,128,2048]{2,1,0:T(8,128)(2,1)}), bf16[8,128,2048]{2,1,0:T(8,128)(2,1)}, u32[]{:S(2)}, u32[]{:S(2)}) %all-to-all-start.1) | async-done | bytes 4194336 | tf_op jit(solution)/shard_map/all_to_all | solution.py:58
  70.1 19.1 %gather_fusion.1 = bf16[2048,2048]{1,0:T(8,128)(2,1)} fusion(bf16[1024,2048]{1,0:T(8,128)(2,1)} %bitcast.15, s32[2048]{0:T(1024)S(1)} %fusion.31), kind=kCustom, calls=%fused_computation.7 | custom fusion | bytes 16785408 | tf_op jit(solution)/shard_map/gather | solution.py:83
  89.1 5.9 %all-to-all-start.2 = ((bf16[4,512,2048]{2,1,0:T(8,128)(2,1)}), bf16[4,512,2048]{2,1,0:T(8,128)(2,1)}, u32[]{:S(2)}, u32[]{:S(2)}) async-start(bf16[4,512,2048]{2,1,0:T(8,128)(2,1)} %bitcast.122), calls=%async_computation.2 | async-start | bytes 16777216 | tf_op jit(solution)/shard_map/all_to_all | solution.py:84
  95.0 1.8 collective-permute-start.1
  96.8 178.5 %all-to-all-done.2 = bf16[4,512,2048]{2,1,0:T(8,128)(2,1)} async-done(((bf16[4,512,2048]{2,1,0:T(8,128)(2,1)}), bf16[4,512,2048]{2,1,0:T(8,128)(2,1)}, u32[]{:S(2)}, u32[]{:S(2)}) %all-to-all-start.2) | async-done | bytes 8388640 | tf_op jit(solution)/shard_map/all_to_all | solution.py:84
  275.3 7.0 %fusion.8 = f32[2048,384]{1,0:T(8,128)S(1)} fusion(bf16[2048,2048]{1,0:T(8,128)(2,1)} %bitcast.21, bf16[1,2048,384]{2,1,0:T(8,128)(2,1)S(1)} %copy-done), kind=kOutput, calls=%fused_computation.27 | convolution fusion | flops 3221225472 | bytes 13107200 | tf_op jit(solution)/shard_map/dot_general | solution.py:86
  282.3 8.6 %multiply_convert_fusion = bf16[2048,384]{1,0:T(8,128)(2,1)S(1)} fusion(f32[2048,384]{1,0:T(8,128)S(1)} %fusion.8, bf16[2048,2048]{1,0:T(8,128)(2,1)} %bitcast.21, bf16[1,2048,384]{2,1,0:T(8,128)(2,1)S(1)} %copy-done.5), kind=kOutput, calls=%fused_computation.21 | convolution fusion | flops 3225944064 | bytes 14680064 | tf_op jit(solution)/shard_map/dot_general | solution.py:87
  290.9 0.1 constant_dynamic-slice_fusion
  291.0 0.1 collective-permute-start
  291.1 0.0 collective-permute-done.1
  291.1 2.5 broadcast_select_fusion.1
  293.6 16.0 %collective-permute-done = bf16[4,256,384]{2,1,0:T(8,128)(2,1)} collective-permute-done((bf16[4,256,384]{2,1,0:T(8,128)(2,1)S(1)}, bf16[4,256,384]{2,1,0:T(8,128)(2,1)}, u32[]{:S(2)}, u32[]{:S(2)}) %collective-permute-start) | collective-permute-done | bytes 786464 | tf_op jit(solution)/shard_map/ppermute | solution.py:16
  309.6 1.7 broadcast_select_fusion.3
  311.3 0.1 pad_maximum_fusion
  311.4 5.0 %convolution_convert_fusion = bf16[1024,2048]{1,0:T(8,128)(2,1)} fusion(bf16[1024,768]{1,0:T(8,128)(2,1)S(1)} %bitcast.128, bf16[384,2048]{1,0:T(8,128)(2,1)S(1)} %get-tuple-element.19, bf16[384,2048]{1,0:T(8,128)(2,1)S(1)} %get-tuple-element.18), kind=kOutput, calls=%fused_computation.16 | convolution fusion | flops 3229614080 | bytes 8912896 | tf_op jit(solution)/shard_map/dot_general | solution.py:95
  316.4 5.1 %all-to-all-start.3 = ((bf16[4,256,2048]{2,1,0:T(8,128)(2,1)}), bf16[4,256,2048]{2,1,0:T(8,128)(2,1)}, u32[]{:S(2)}, u32[]{:S(2)}) async-start(bf16[4,256,2048]{2,1,0:T(8,128)(2,1)} %bitcast.126), calls=%async_computation.3 | async-start | bytes 8388608 | tf_op jit(solution)/shard_map/all_to_all | solution.py:99
  321.5 0.2 rev.3
  321.7 0.6 iota_reduce_fusion.1
  322.4 6.5 %gather_fusion.5 = s32[1024]{0:T(1024)S(1)} fusion(s32[1024,8]{0,1:T(8,128)S(1)} %get-tuple-element.17, s32[1024]{0:T(1024)S(1)} %bitcast.118), kind=kCustom, calls=%fused_computation.2.clone | custom fusion | bytes 16384 | tf_op jit(solution)/shard_map/jit(take_along_axis)/gather | solution.py:106
  328.9 6.5 %gather_fusion.4 = s32[1024]{0:T(1024)S(1)} fusion(s32[1024,8]{0,1:T(8,128)S(1)} %slice.49, s32[1024]{0:T(1024)S(1)} %bitcast.119), kind=kCustom, calls=%fused_computation.clone | custom fusion | bytes 16384 | tf_op jit(solution)/shard_map/jit(take_along_axis)/gather | solution.py:111
  335.4 0.6 iota_reduce_fusion
  336.2 6.5 %gather_fusion.7 = s32[1024]{0:T(1024)S(1)} fusion(s32[1024,8]{0,1:T(8,128)S(1)} %slice.49, s32[1024]{0:T(1024)S(1)} %bitcast.116), kind=kCustom, calls=%fused_computation.3.clone | custom fusion | bytes 16384 | tf_op jit(solution)/shard_map/jit(take_along_axis)/gather | solution.py:111
  342.7 6.5 %gather_fusion.8 = s32[1024]{0:T(1024)S(1)} fusion(s32[1024,8]{0,1:T(8,128)S(1)} %get-tuple-element.17, s32[1024]{0:T(1024)S(1)} %bitcast.117), kind=kCustom, calls=%fused_computation.4.clone | custom fusion | bytes 16384 | tf_op jit(solution)/shard_map/jit(take_along_axis)/gather | solution.py:106
  349.2 9.1 %gather_fusion.6 = s32[1024]{0:T(1024)S(1)} fusion(s32[1024,2]{0,1:T(2,128)S(1)} %bitcast.114, s32[1024]{0:T(1024)S(1)} %bitcast.121), kind=kCustom, calls=%fused_computation.1.clone | custom fusion | bytes 16384 | tf_op jit(solution)/shard_map/jit(take_along_axis)/gather | solution.py:108
  358.3 0.1 compare_select_fusion.7
  358.5 9.1 %gather_fusion.9 = s32[1024]{0:T(1024)S(1)} fusion(s32[1024,2]{0,1:T(2,128)S(1)} %bitcast.115, s32[1024]{0:T(1024)S(1)} %bitcast.120), kind=kCustom, calls=%fused_computation.5.clone | custom fusion | bytes 16384 | tf_op jit(solution)/shard_map/jit(take_along_axis)/gather | solution.py:108
  367.6 0.1 compare_select_fusion.6
  367.6 45.3 %all-to-all-done.3 = bf16[4,256,2048]{2,1,0:T(8,128)(2,1)} async-done(((bf16[4,256,2048]{2,1,0:T(8,128)(2,1)}), bf16[4,256,2048]{2,1,0:T(8,128)(2,1)}, u32[]{:S(2)}, u32[]{:S(2)}) %all-to-all-start.3) | async-done | bytes 4194336 | tf_op jit(solution)/shard_map/all_to_all | solution.py:99
  413.0 11.6 %gather_fusion.2 = bf16[1024,2048]{1,0:T(8,128)(2,1)} fusion(bf16[1024,2048]{1,0:T(8,128)(2,1)} %bitcast.28, s32[1024]{0:T(1024)S(1)} %broadcast_clamp_fusion.1), kind=kCustom, calls=%fused_computation.8 | custom fusion | bytes 8392704 | tf_op jit(solution)/shard_map/gather | solution.py:113
  424.5 11.6 %gather_fusion.3 = bf16[1024,2048]{1,0:T(8,128)(2,1)} fusion(bf16[1024,2048]{1,0:T(8,128)(2,1)} %bitcast.28, s32[1024]{0:T(1024)S(1)} %broadcast_clamp_fusion), kind=kCustom, calls=%fused_computation.9 | custom fusion | bytes 8392704 | tf_op jit(solution)/shard_map/gather | solution.py:113
  436.1 4.3 fusion.1
  440.4 0.0 copy-start.1
  440.4 54.7 %all_to_all.25 = bf16[8,128,2048]{2,1,0:T(8,128)(2,1)S(1)} all-to-all(bf16[8,128,2048]{2,1,0:T(8,128)(2,1)S(1)} %fusion.1), channel_id=1, replica_groups=mesh['grp'=8,'loc'=4] {'grp'}, dimensions={0} | all-to-all | bytes 8388608 | tf_op jit(solution)/shard_map/all_to_all | solution.py:117
  495.1 1.6 fusion.6
  (47 shorter events, 0.6 us)
Async XLA Ops:
  0.0 275.3 %copy-start = (bf16[1,2048,384]{2,1,0:T(8,128)(2,1)S(1)}, bf16[1,2048,384]{2,1,0:T(8,128)(2,1)}, u32[]{:S(2)}) copy-start(bf16[1,2048,384]{2,1,0:T(8,128)(2,1)} %param.13) | copy-start | bytes 4718596
  1.0 10.7 %copy-start.4 = (bf16[2048]{0:T(1024)(128)(2,1)S(1)}, bf16[2048]{0:T(1024)(128)(2,1)}, u32[]{:S(2)}) copy-start(bf16[2048]{0:T(1024)(128)(2,1)} %param.12) | copy-start | bytes 12292
  1.0 10.8 %copy-start.2 = (bf16[128,2048]{1,0:T(8,128)(2,1)S(1)}, bf16[128,2048]{1,0:T(8,128)(2,1)}, u32[]{:S(2)}) copy-start(bf16[128,2048]{1,0:T(8,128)(2,1)} %param.11) | copy-start | bytes 1572868
  6.3 10.0 %all-to-all-start = ((bf16[8,128,16]{1,2,0:T(8,128)(2,1)}), bf16[8,128,16]{1,2,0:T(8,128)(2,1)S(1)}, u32[]{:S(2)}, u32[]{:S(2)}) async-start(bf16[8,128,16]{1,2,0:T(8,128)(2,1)} %select_convert_fusion), calls=%async_computation | async-start | bytes 65536 | tf_op jit(solution)/shard_map/all_to_all | solution.py:59
  16.3 53.7 %all-to-all-start.1 = ((bf16[8,128,2048]{2,1,0:T(8,128)(2,1)}), bf16[8,128,2048]{2,1,0:T(8,128)(2,1)}, u32[]{:S(2)}, u32[]{:S(2)}) async-start(bf16[8,128,2048]{2,1,0:T(8,128)(2,1)} %bitcast.123), calls=%async_computation.1 | async-start | bytes 8388608 | tf_op jit(solution)/shard_map/all_to_all | solution.py:58
  89.1 186.2 %all-to-all-start.2 = ((bf16[4,512,2048]{2,1,0:T(8,128)(2,1)}), bf16[4,512,2048]{2,1,0:T(8,128)(2,1)}, u32[]{:S(2)}, u32[]{:S(2)}) async-start(bf16[4,512,2048]{2,1,0:T(8,128)(2,1)} %bitcast.122), calls=%async_computation.2 | async-start | bytes 16777216 | tf_op jit(solution)/shard_map/all_to_all | solution.py:84
  95.0 196.1 %collective-permute-start.1 = (bf16[384,2048]{1,0:T(8,128)(2,1)}, bf16[384,2048]{1,0:T(8,128)(2,1)}, u32[]{:S(2)}, u32[]{:S(2)}) collective-permute-start(bf16[384,2048]{1,0:T(8,128)(2,1)} %bitcast.131), channel_id=1, source_target_pairs={{0,1},{1,0},{2,3},{3,2},{4,5},{5,4},{6,7},{7,6},{8,9},{9,8},{10,11... | collective-permute-start | bytes 4718600 | tf_op jit(solution)/shard_map/ppermute | solution.py:16
  275.3 7.0 %copy-start.5 = (bf16[1,2048,384]{2,1,0:T(8,128)(2,1)S(1)}, bf16[1,2048,384]{2,1,0:T(8,128)(2,1)}, u32[]{:S(2)}) copy-start(bf16[1,2048,384]{2,1,0:T(8,128)(2,1)} %param.14) | copy-start | bytes 4718596
  290.9 2.7 copy-start.3
  291.0 18.6 %collective-permute-start = (bf16[4,256,384]{2,1,0:T(8,128)(2,1)S(1)}, bf16[4,256,384]{2,1,0:T(8,128)(2,1)}, u32[]{:S(2)}, u32[]{:S(2)}) collective-permute-start(bf16[4,256,384]{2,1,0:T(8,128)(2,1)S(1)} %constant_dynamic-slice_fusion), channel_id=1, source_target_pairs={{0,1},{1,0},{2,3},{3,2},{4,5},{5,4},{6,7},{7,6},{8,9},{9,8},{10,11... | collective-permute-start | bytes 2359304 | tf_op jit(solution)/shard_map/ppermute | solution.py:16
  316.4 96.6 %all-to-all-start.3 = ((bf16[4,256,2048]{2,1,0:T(8,128)(2,1)}), bf16[4,256,2048]{2,1,0:T(8,128)(2,1)}, u32[]{:S(2)}, u32[]{:S(2)}) async-start(bf16[4,256,2048]{2,1,0:T(8,128)(2,1)} %bitcast.126), calls=%async_computation.3 | async-start | bytes 8388608 | tf_op jit(solution)/shard_map/all_to_all | solution.py:99
  440.4 56.3 %copy-start.1 = (bf16[1,2048,384]{2,1,0:T(8,128)(2,1)S(1)}, bf16[1,2048,384]{2,1,0:T(8,128)(2,1)}, u32[]{:S(2)}) copy-start(bf16[1,2048,384]{2,1,0:T(8,128)(2,1)} %param.13) | copy-start | bytes 4718596
where the time goes:
time: 497 us
  waiting for transfers between devices  271 us (55%)
  local copies, waits for them, and re-layouts  109 us (22%)
  blocking collectives  54.7 us (11%)
  matrix products  25.4 us (5%)
  starting transfers between devices  22.6 us (5%)
  other arithmetic  13.6 us (3%)
    all_to_all x1, waiting for transfers between devices, shards(): lax.all_to_all(outgoing, 'loc', split_axis=0, concat_axis=0, tiled=True)  179 us
    all_to_all x1, blocking collectives, shards(): lax.all_to_all(group_sum, 'grp', split_axis=0, concat_axis=0, tiled=True)  54.7 us
    all_to_all x1, waiting for transfers between devices, shards(): lax.all_to_all(result, 'loc', split_axis=0, concat_axis=0, tiled=True)  45.3 us
    all_to_all x1, waiting for transfers between devices, shards(): lax.all_to_all(packed, 'grp', split_axis=0, concat_axis=0, tiled=True)  30.3 us
    gather x2, local copies, waits for them, and re-layouts, pick_term(): return weight[:, None] * flat_returned[row_pick].astype(jnp.float32)  23.1 us
    gather x1, local copies, waits for them, and re-layouts, shards(): arrived[source_slot].reshape(local_count, expert_rows, model_width)  19.1 us
    gather x2, local copies, waits for them, and re-layouts, pick_term(): rank_pick = jnp.take_along_axis(ranking, local_pick[:, None], axis=1)[:, 0]  18.2 us
    ppermute x2, waiting for transfers between devices, from_partner(): return lax.ppermute(value, axis, pairs)  16 us
  transfers between devices with their start and end apart: 6, of which 5 were waited for; matrix products, arithmetic and copies ran while one was open for 17% of the time, Pallas kernels for 0%

commit v1 on v0

--- a/solution.py
+++ b/solution.py
@@ -1,6 +1,8 @@
 import jax
 import jax.numpy as jnp
 from jax import lax
+from jax.experimental import pallas as pl
+from jax.experimental.pallas import tpu as pltpu
 from jax.sharding import PartitionSpec as P
 
 GTOP = 4
@@ -22,7 +24,7 @@
     return jnp.concatenate([lower_part, upper_part], axis=axis_index)
 
 
-def shards(tokens, norm_gain, w_gate, w_up, w_down, expert_ids, gate_num):
+def routed(tokens, norm_gain, w_gate, w_up, w_down, expert_ids, gate_num):
     group_count = lax.axis_size("grp")
     local_count = lax.axis_size("loc")
     rows_dev, model_width = tokens.shape
@@ -123,6 +125,329 @@
     return (inputs_float + mixed_sum).astype(jnp.bfloat16)
 
 
+MESH = pl.DeviceIdType.MESH
+Z, X, Y, S, FA, FB, R1, R2A, R2B, R3X, R3Y, R4 = 0, 1, 2, 3, 7, 8, 9, 13, 14, 15, 16, 17
+KINDS = 18
+
+
+def flip(value, bit, unit):
+    digit = (value // unit) % 2
+    return value + unit * ((digit + bit) % 2 - digit)
+
+
+def fused_kernel(
+    tokens_ref, gain_ref, w_gate_ref, w_up_ref, w_down_ref, ids_ref, nums_ref, out_ref,
+    rows, sums, from_sibling, diag_in, near_in, z_in, w_in, num_all,
+    send_sem, recv_sem, num_send, num_recv,
+):
+    grp, loc = lax.axis_index("grp"), lax.axis_index("loc")
+    n_rows, width = tokens_ref.shape
+    half = n_rows // 2
+    hidden_units = w_gate_ref.shape[2]
+    experts = num_all.shape[1]
+    sibling = (flip(grp, 1, 1), loc)
+    along_x = (flip(grp, 1, 2), loc)
+    along_y = (flip(grp, 1, 4), loc)
+    me = grp * 4 + loc
+    everyone = 32
+
+    barrier = pltpu.get_barrier_semaphore()
+
+    @pl.loop(1, everyone)
+    def _(i):
+        other = (me + i) % everyone
+        pl.semaphore_signal(barrier, 1, device_id=(other // 4, other % 4), device_id_type=MESH)
+
+    inputs = tokens_ref[...].astype(jnp.float32)
+    inv_scale = lax.rsqrt(jnp.mean(inputs * inputs, axis=-1, keepdims=True) + epsilon)
+    rows[0, pl.ds(0, n_rows), :] = (
+        inputs * inv_scale * gain_ref[...].astype(jnp.float32)
+    ).astype(jnp.bfloat16)
+    expert_row = lax.broadcasted_iota(jnp.int32, (experts, n_rows), 0)
+    numerators = jnp.zeros((experts, n_rows), jnp.int32)
+    for k in range(ids_ref.shape[0]):
+        numerators += jnp.where(ids_ref[k : k + 1, :] == expert_row, nums_ref[k : k + 1, :], 0)
+    num_all[me] = numerators.astype(jnp.float32).astype(jnp.bfloat16)
+    pl.semaphore_wait(barrier, everyone - 1)
+
+    def remote(kind, j, source, target, device):
+        return pltpu.make_async_remote_copy(
+            src_ref=source,
+            dst_ref=target,
+            send_sem=send_sem.at[kind * 4 + j],
+            recv_sem=recv_sem.at[kind * 4 + j],
+            device_id=device,
+            device_id_type=MESH,
+        )
+
+    own, other_core = pl.ds(0, n_rows), pl.ds(n_rows, n_rows)
+    first, second = pl.ds(0, half), pl.ds(half, half)
+
+    def partner(j):
+        return (grp, flip(flip(loc, j % 2, 1), j // 2, 2))
+
+    def copy_z(j):
+        return remote(Z, j, rows.at[0, own], rows.at[4 * j, own], partner(j))
+
+    def copy_x(j):
+        return remote(X, j, rows.at[4 * j, own], rows.at[4 * j + 1, own], along_x)
+
+    def copy_y(j):
+        return remote(Y, j, rows.at[4 * j, own], rows.at[4 * j + 2, own], along_y)
+
+    def copy_s(j, q):
+        t = 4 * j + q
+        return remote(S + q, j, rows.at[t, own], rows.at[t, other_core], sibling)
+
+    def copy_fa(j):
+        return remote(FA, j, rows.at[4 * j + 1, first], rows.at[4 * j + 3, first], along_y)
+
+    def copy_fb(j):
+        return remote(FB, j, rows.at[4 * j + 2, second], rows.at[4 * j + 3, second], along_x)
+
+    def copy_r1(j, q):
+        t = 4 * j + q
+        return remote(R1 + q, j, rows.at[t, other_core], from_sibling.at[t], sibling)
+
+    def copy_r2a(j):
+        return remote(R2A, j, sums.at[4 * j + 3, first], diag_in.at[j, first], along_x)
+
+    def copy_r2b(j):
+        return remote(R2B, j, sums.at[4 * j + 3, second], diag_in.at[j, second], along_y)
+
+    def copy_r3x(j):
+        return remote(R3X, j, sums.at[4 * j + 1], near_in.at[j, 0], along_x)
+
+    def copy_r3y(j):
+        return remote(R3Y, j, sums.at[4 * j + 2], near_in.at[j, 1], along_y)
+
+    def copy_r4(j):
+        return remote(R4, j, sums.at[4 * j], z_in.at[j], partner(j))
+
+    def numerator_copy(source, target, device):
+        return pltpu.make_async_remote_copy(
+            src_ref=source,
+            dst_ref=target,
+            send_sem=num_send,
+            recv_sem=num_recv,
+            device_id=device,
+            device_id_type=MESH,
+        )
+
+    def spread(j):
+        copy_x(j).start()
+        copy_y(j).start()
+        copy_s(j, 0).start()
+
+    def forward(j):
+        copy_x(j).wait_recv()
+        copy_fa(j).start()
+        copy_s(j, 1).start()
+        copy_y(j).wait_recv()
+        copy_fb(j).start()
+        copy_s(j, 2).start()
+
+    def forward_diagonal(j):
+        copy_fa(j).wait_recv()
+        copy_fb(j).wait_recv()
+        copy_s(j, 3).start()
+
+    def add(t, extra=(), place=None):
+        place = pl.ds(0, n_rows) if place is None else place
+        total = sums[t, place, :].astype(jnp.float32)
+        total += from_sibling[t, place, :].astype(jnp.float32)
+        for term in extra:
+            total += term[place, :].astype(jnp.float32)
+        sums[t, place, :] = total.astype(jnp.bfloat16)
+
+    def reduce_diagonal(j):
+        copy_r1(j, 3).wait_recv()
+        add(4 * j + 3)
+        copy_r2a(j).start()
+        copy_r2b(j).start()
+
+    def reduce_near(j):
+        copy_r1(j, 1).wait_recv()
+        add(4 * j + 1, (), first)
+        copy_r2b(j).wait_recv()
+        add(4 * j + 1, (diag_in.at[j],), second)
+        copy_r3x(j).start()
+        copy_r1(j, 2).wait_recv()
+        add(4 * j + 2, (), second)
+        copy_r2a(j).wait_recv()
+        add(4 * j + 2, (diag_in.at[j],), first)
+        copy_r3y(j).start()
+
+    def reduce_plane(j):
+        copy_r1(j, 0).wait_recv()
+        copy_r3x(j).wait_recv()
+        copy_r3y(j).wait_recv()
+        add(4 * j, (near_in.at[j, 0], near_in.at[j, 1]))
+
+    for j in (1, 2, 3):
+        copy_z(j).start()
+    spread(0)
+
+    @pl.loop(1, everyone)
+    def _(i):
+        other = (me + i) % everyone
+        numerator_copy(num_all.at[me], num_all.at[me], (other // 4, other % 4)).start()
+
+    w_in[:, :hidden_units] = w_gate_ref[0]
+    w_in[:, hidden_units:] = w_up_ref[0]
+    forward(0)
+    copy_z(1).wait_recv()
+    spread(1)
+    numerator_copy(
+        num_all.at[pl.ds(0, everyone - 1)], num_all.at[pl.ds(0, everyone - 1)], sibling
+    ).wait_recv()
+
+    own_expert = grp * 2 + loc // 2
+    pick = (expert_row == own_expert).astype(jnp.float32).astype(jnp.bfloat16)
+
+    def weights_of(j, q, core_flip):
+        source = flip(flip(flip(grp, core_flip, 1), q % 2, 2), q // 2, 4)
+        place = source * 4 + partner(j)[1]
+        return lax.dot_general(
+            num_all[place], pick, (((0,), (0,)), ((), ())), preferred_element_type=jnp.float32
+        )[:, :1] * (1.0 / denominator)
+
+    @pl.loop(0, 16)
+    def _(t):
+        j, q = t // 4, t % 4
+
+        @pl.when(q == 0)
+        def _():
+            @pl.when(j >= 2)
+            def _():
+                reduce_plane(j - 2)
+
+                @pl.when(j >= 3)
+                def _():
+                    copy_r4(j - 2).start()
+
+            copy_s(j, 0).wait_recv()
+
+        @pl.when(q == 1)
+        def _():
+            @pl.when(j >= 1)
+            def _():
+                reduce_diagonal(j - 1)
+
+            forward_diagonal(j)
+            copy_s(j, 1).wait_recv()
+
+        @pl.when(q == 2)
+        def _():
+            @pl.when(j >= 1)
+            def _():
+                reduce_near(j - 1)
+
+            copy_s(j, 2).wait_recv()
+
+        @pl.when(q == 3)
+        def _():
+            @pl.when(j < 3)
+            def _():
+                forward(j + 1)
+
+            @pl.when(j < 2)
+            def _():
+                copy_z(j + 2).wait_recv()
+                spread(j + 2)
+
+            copy_s(j, 3).wait_recv()
+
+        both = jnp.dot(rows[t], w_in[...], preferred_element_type=jnp.float32)
+        gate_act, up_act = both[:, :hidden_units], both[:, hidden_units:]
+        hidden = (jax.nn.silu(gate_act) * up_act).astype(jnp.bfloat16)
+        weight = jnp.concatenate([weights_of(j, q, 0), weights_of(j, q, 1)], axis=0)
+        step = width // 4
+        for part in range(4):
+            columns = pl.ds(part * step, step)
+            result = jnp.dot(
+                hidden, w_down_ref[0, :, columns], preferred_element_type=jnp.float32
+            )
+            result = (result * weight).astype(jnp.bfloat16)
+            sums[t, :, columns] = result[:n_rows]
+            rows[t, other_core, columns] = result[n_rows:]
+        for which in range(4):
+            @pl.when(q == which)
+            def _():
+                copy_r1(j, which).start()
+
+    reduce_diagonal(3)
+    reduce_plane(2)
+    copy_r4(2).start()
+    reduce_near(3)
+    reduce_plane(3)
+    copy_r4(3).start()
+    total = tokens_ref[...].astype(jnp.float32) + sums[0].astype(jnp.float32)
+    for j in (1, 2, 3):
+        copy_r4(j).wait_recv()
+        total += z_in[j].astype(jnp.float32)
+    out_ref[...] = total.astype(jnp.bfloat16)
+
+    @pl.loop(0, 4)
+    def _(j):
+        @pl.when(j > 0)
+        def _():
+            copy_z(j).wait_send()
+            copy_r4(j).wait_send()
+
+        copy_x(j).wait_send()
+        copy_y(j).wait_send()
+        for q in range(4):
+            copy_s(j, q).wait_send()
+            copy_r1(j, q).wait_send()
+        for make in (copy_fa, copy_fb, copy_r2a, copy_r2b, copy_r3x, copy_r3y):
+            make(j).wait_send()
+
+    numerator_copy(
+        num_all.at[pl.ds(0, everyone - 1)], num_all.at[pl.ds(0, everyone - 1)], sibling
+    ).wait_send()
+
+
+def fused(tokens, norm_gain, w_gate, w_up, w_down, expert_ids, gate_num):
+    n_rows, width = tokens.shape
+    hidden_units = w_gate.shape[2]
+    bf16 = jnp.bfloat16
+    return pl.pallas_call(
+        fused_kernel,
+        out_shape=jax.ShapeDtypeStruct(tokens.shape, tokens.dtype),
+        in_specs=[pl.BlockSpec(memory_space=pltpu.VMEM)] * 7,
+        out_specs=pl.BlockSpec(memory_space=pltpu.VMEM),
+        scratch_shapes=[
+            pltpu.VMEM((16, 2 * n_rows, width), bf16),
+            pltpu.VMEM((16, n_rows, width), bf16),
+            pltpu.VMEM((16, n_rows, width), bf16),
+            pltpu.VMEM((4, n_rows, width), bf16),
+            pltpu.VMEM((4, 2, n_rows, width), bf16),
+            pltpu.VMEM((4, n_rows, width), bf16),
+            pltpu.VMEM((width, 2 * hidden_units), bf16),
+            pltpu.VMEM((32, 16, n_rows), bf16),
+            pltpu.SemaphoreType.DMA((KINDS * 4,)),
+            pltpu.SemaphoreType.DMA((KINDS * 4,)),
+            pltpu.SemaphoreType.DMA,
+            pltpu.SemaphoreType.DMA,
+        ],
+        compiler_params=pltpu.CompilerParams(
+            collective_id=0, has_side_effects=True, vmem_limit_bytes=60 * 2**20
+        ),
+        cost_estimate=pl.CostEstimate(
+            flops=2 * 32 * n_rows * width * hidden_units * 3,
+            bytes_accessed=2 * width * hidden_units * 3,
+            transcendentals=32 * n_rows * hidden_units,
+        ),
+    )(tokens, norm_gain.reshape(1, width), w_gate, w_up, w_down, expert_ids.T, gate_num.T)
+
+
+def shards(tokens, *others):
+    if (lax.axis_size("grp"), lax.axis_size("loc")) == (8, 4):
+        return fused(tokens, *others)
+    return routed(tokens, *others)
+
+
 def solution(mesh):
     return jax.shard_map(
         shards,

time: 497 us -> 210 us (0.42)
  the two profiles are of different devices: /device:TPU:0 before, /device:TPU:8 now
where the time goes in v1:
time: 210 us; the launch traced here: 209 us
  Pallas kernels  206 us (98%)
  local copies, waits for them, and re-layouts  3.17 us (2%)
    pallas_call x1, Pallas kernels, fused(): pl.pallas_call(fused_kernel, out_shape=jax.ShapeDtypeStruct(tokens.shape,...  206 us

profile of v1, /device:TPU:8, one launch (start us, length us, event | category | flops | bytes accessed | tf_op | source)
XLA Modules:
  0.0 209.4 jit_solution(11627401391072819790)
XLA Ops:
  0.0 1.3 reshape.3.gain_ref
  1.3 206.2 %shard_map.73 = bf16[128,2048]{1,0:T(8,128)(2,1)} custom-call(bf16[128,2048]{1,0:T(8,128)(2,1)} %tokens_ref.1, bf16[1,2048]{1,0:T(2,128)(2,1)} %reshape.3.gain_ref, bf16[1,2048,384]{2,1,0:T(8,128)(2,1)} %w_gate_ref.1, bf16[1,2048,384]{2,1,0:T(8,128)(2,1)} %w_up_ref.1, bf16[1,384,2048]{2,1,0:T(8,128)(2,1)} %w_down_ref.1, s32[8,128]{1,0:T(8,128)} %bitcast.2, ...), custom_call_target="tpu_custom_call" | custom-call | flops 19327352832 | bytes 4718592 | tf_op jit(solution)/shard_map/pallas_call | solution.py:415
  207.5 1.9 copy.9

commit v2 on v1

--- a/solution.py
+++ b/solution.py
@@ -138,7 +138,7 @@
 def fused_kernel(
     tokens_ref, gain_ref, w_gate_ref, w_up_ref, w_down_ref, ids_ref, nums_ref, out_ref,
     rows, sums, from_sibling, diag_in, near_in, z_in, w_in, num_all,
-    send_sem, recv_sem, num_send, num_recv,
+    send_sem, recv_sem, z_send, num_send, num_recv,
 ):
     grp, loc = lax.axis_index("grp"), lax.axis_index("loc")
     n_rows, width = tokens_ref.shape
@@ -150,6 +150,16 @@
     along_y = (flip(grp, 1, 4), loc)
     me = grp * 4 + loc
     everyone = 32
+    upper = loc // 2
+    mirrored = loc + upper * (3 - 2 * loc)
+    outer, inner, far_inner = 3 * upper, 1 + upper, 2 - upper
+
+    def plane(i):
+        from_end = (i // 2) * i + (1 - i // 2) * ((mirrored + i) % 2)
+        return from_end + upper * (3 - 2 * from_end)
+
+    def worked(k):
+        return plane((k + 1) % 4)
 
     barrier = pltpu.get_barrier_semaphore()
 
@@ -160,7 +170,7 @@
 
     inputs = tokens_ref[...].astype(jnp.float32)
     inv_scale = lax.rsqrt(jnp.mean(inputs * inputs, axis=-1, keepdims=True) + epsilon)
-    rows[0, pl.ds(0, n_rows), :] = (
+    rows[4 * loc, pl.ds(0, n_rows), :] = (
         inputs * inv_scale * gain_ref[...].astype(jnp.float32)
     ).astype(jnp.bfloat16)
     expert_row = lax.broadcasted_iota(jnp.int32, (experts, n_rows), 0)
@@ -183,11 +193,15 @@
     own, other_core = pl.ds(0, n_rows), pl.ds(n_rows, n_rows)
     first, second = pl.ds(0, half), pl.ds(half, half)
 
-    def partner(j):
-        return (grp, flip(flip(loc, j % 2, 1), j // 2, 2))
-
-    def copy_z(j):
-        return remote(Z, j, rows.at[0, own], rows.at[4 * j, own], partner(j))
+    def copy_z(j, index, target):
+        return pltpu.make_async_remote_copy(
+            src_ref=rows.at[4 * j, own],
+            dst_ref=rows.at[4 * j, own],
+            send_sem=z_send.at[index],
+            recv_sem=recv_sem.at[Z * 4 + j],
+            device_id=(grp, target),
+            device_id_type=MESH,
+        )
 
     def copy_x(j):
         return remote(X, j, rows.at[4 * j, own], rows.at[4 * j + 1, own], along_x)
@@ -222,7 +236,24 @@
         return remote(R3Y, j, sums.at[4 * j + 2], near_in.at[j, 1], along_y)
 
     def copy_r4(j):
-        return remote(R4, j, sums.at[4 * j], z_in.at[j], partner(j))
+        return pltpu.make_async_remote_copy(
+            src_ref=sums.at[4 * j],
+            dst_ref=z_in.at[loc],
+            send_sem=send_sem.at[R4 * 4 + j],
+            recv_sem=recv_sem.at[R4 * 4 + loc],
+            device_id=(grp, j),
+            device_id_type=MESH,
+        )
+
+    def arrival_r4(j):
+        return pltpu.make_async_remote_copy(
+            src_ref=z_in.at[j],
+            dst_ref=z_in.at[j],
+            send_sem=send_sem.at[R4 * 4 + j],
+            recv_sem=recv_sem.at[R4 * 4 + j],
+            device_id=(grp, j),
+            device_id_type=MESH,
+        )
 
     def numerator_copy(source, target, device):
         return pltpu.make_async_remote_copy(
@@ -284,9 +315,27 @@
         copy_r3y(j).wait_recv()
         add(4 * j, (near_in.at[j, 0], near_in.at[j, 1]))
 
-    for j in (1, 2, 3):
-        copy_z(j).start()
-    spread(0)
+    is_inner = mirrored == 1
+
+    def take_plane(i, target):
+        copy_z(plane(i), 1 + i, target).wait_recv()
+
+        @pl.when(is_inner)
+        def _():
+            copy_z(plane(i), 1 + i, target).start()
+
+        spread(plane(i))
+
+    @pl.when(is_inner)
+    def _():
+        copy_z(loc, 0, outer).start()
+        copy_z(loc, 1, far_inner).start()
+
+    @pl.when(mirrored == 0)
+    def _():
+        copy_z(loc, 0, inner).start()
+
+    spread(loc)
 
     @pl.loop(1, everyone)
     def _(i):
@@ -295,9 +344,12 @@
 
     w_in[:, :hidden_units] = w_gate_ref[0]
     w_in[:, hidden_units:] = w_up_ref[0]
-    forward(0)
-    copy_z(1).wait_recv()
-    spread(1)
+    forward(loc)
+    take_plane(1, far_inner)
+    take_plane(2, outer)
+    forward_diagonal(loc)
+    forward(plane(1))
+    take_plane(3, outer)
     numerator_copy(
         num_all.at[pl.ds(0, everyone - 1)], num_all.at[pl.ds(0, everyone - 1)], sibling
     ).wait_recv()
@@ -307,54 +359,51 @@
 
     def weights_of(j, q, core_flip):
         source = flip(flip(flip(grp, core_flip, 1), q % 2, 2), q // 2, 4)
-        place = source * 4 + partner(j)[1]
+        place = source * 4 + j
         return lax.dot_general(
             num_all[place], pick, (((0,), (0,)), ((), ())), preferred_element_type=jnp.float32
         )[:, :1] * (1.0 / denominator)
 
     @pl.loop(0, 16)
-    def _(t):
-        j, q = t // 4, t % 4
+    def _(step):
+        k, q = step // 4, step % 4
+        j = worked(k)
+        t = 4 * j + q
 
         @pl.when(q == 0)
         def _():
-            @pl.when(j >= 2)
+            @pl.when(k >= 2)
             def _():
-                reduce_plane(j - 2)
-
-                @pl.when(j >= 3)
-                def _():
-                    copy_r4(j - 2).start()
+                reduce_plane(worked(k - 2))
+                copy_r4(worked(k - 2)).start()
 
             copy_s(j, 0).wait_recv()
 
         @pl.when(q == 1)
         def _():
-            @pl.when(j >= 1)
+            @pl.when(k >= 1)
             def _():
-                reduce_diagonal(j - 1)
-
-            forward_diagonal(j)
+                reduce_diagonal(worked(k - 1))
+
+            @pl.when(k < 3)
+            def _():
+                forward_diagonal(j)
+
             copy_s(j, 1).wait_recv()
 
         @pl.when(q == 2)
         def _():
-            @pl.when(j >= 1)
+            @pl.when(k >= 1)
             def _():
-                reduce_near(j - 1)
+                reduce_near(worked(k - 1))
 
             copy_s(j, 2).wait_recv()
 
         @pl.when(q == 3)
         def _():
-            @pl.when(j < 3)
+            @pl.when(k < 2)
             def _():
-                forward(j + 1)
-
-            @pl.when(j < 2)
-            def _():
-                copy_z(j + 2).wait_recv()
-                spread(j + 2)
+                forward(plane(k + 2))
 
             copy_s(j, 3).wait_recv()
 
@@ -362,9 +411,9 @@
         gate_act, up_act = both[:, :hidden_units], both[:, hidden_units:]
         hidden = (jax.nn.silu(gate_act) * up_act).astype(jnp.bfloat16)
         weight = jnp.concatenate([weights_of(j, q, 0), weights_of(j, q, 1)], axis=0)
-        step = width // 4
+        piece = width // 4
         for part in range(4):
-            columns = pl.ds(part * step, step)
+            columns = pl.ds(part * piece, piece)
             result = jnp.dot(
                 hidden, w_down_ref[0, :, columns], preferred_element_type=jnp.float32
             )
@@ -376,25 +425,30 @@
             def _():
                 copy_r1(j, which).start()
 
-    reduce_diagonal(3)
-    reduce_plane(2)
-    copy_r4(2).start()
-    reduce_near(3)
-    reduce_plane(3)
-    copy_r4(3).start()
-    total = tokens_ref[...].astype(jnp.float32) + sums[0].astype(jnp.float32)
-    for j in (1, 2, 3):
-        copy_r4(j).wait_recv()
-        total += z_in[j].astype(jnp.float32)
+    reduce_diagonal(loc)
+    reduce_plane(worked(2))
+    copy_r4(worked(2)).start()
+    reduce_near(loc)
+    reduce_plane(loc)
+    total = tokens_ref[...].astype(jnp.float32) + sums[4 * loc].astype(jnp.float32)
+    for i in (1, 2, 3):
+        arrival_r4(plane(i)).wait_recv()
+        total += z_in[plane(i)].astype(jnp.float32)
     out_ref[...] = total.astype(jnp.bfloat16)
+
+    copy_z(loc, 0, outer).wait_send()
+
+    @pl.when(is_inner)
+    def _():
+        copy_z(loc, 1, far_inner).wait_send()
+        for i in (1, 2, 3):
+            copy_z(plane(i), 1 + i, outer).wait_send()
+
+    for i in (1, 2, 3):
+        copy_r4(plane(i)).wait_send()
 
     @pl.loop(0, 4)
     def _(j):
-        @pl.when(j > 0)
-        def _():
-            copy_z(j).wait_send()
-            copy_r4(j).wait_send()
-
         copy_x(j).wait_send()
         copy_y(j).wait_send()
         for q in range(4):
@@ -428,6 +482,7 @@
             pltpu.VMEM((32, 16, n_rows), bf16),
             pltpu.SemaphoreType.DMA((KINDS * 4,)),
             pltpu.SemaphoreType.DMA((KINDS * 4,)),
+            pltpu.SemaphoreType.DMA((5,)),
             pltpu.SemaphoreType.DMA,
             pltpu.SemaphoreType.DMA,
         ],

time: 210 us -> 167 us (0.80)
  the two profiles are of different devices: /device:TPU:8 before, /device:TPU:0 now
where the time goes in v2:
time: 167 us; the launch traced here: 166 us
  Pallas kernels  163 us (98%)
  local copies, waits for them, and re-layouts  3.17 us (2%)
    pallas_call x1, Pallas kernels, fused(): pl.pallas_call(fused_kernel, out_shape=jax.ShapeDtypeStruct(tokens.shape,...  163 us

profile of v2, /device:TPU:0, one launch (start us, length us, event | category | flops | bytes accessed | tf_op | source)
XLA Modules:
  0.0 166.4 jit_solution(7913288184259226469)
XLA Ops:
  0.0 1.3 reshape.3.gain_ref
  1.3 163.3 %shard_map.73 = bf16[128,2048]{1,0:T(8,128)(2,1)} custom-call(bf16[128,2048]{1,0:T(8,128)(2,1)} %tokens_ref.1, bf16[1,2048]{1,0:T(2,128)(2,1)} %reshape.3.gain_ref, bf16[1,2048,384]{2,1,0:T(8,128)(2,1)} %w_gate_ref.1, bf16[1,2048,384]{2,1,0:T(8,128)(2,1)} %w_up_ref.1, bf16[1,384,2048]{2,1,0:T(8,128)(2,1)} %w_down_ref.1, s32[8,128]{1,0:T(8,128)} %bitcast.2, ...), custom_call_target="tpu_custom_call" | custom-call | flops 19327352832 | bytes 4718592 | tf_op jit(solution)/shard_map/pallas_call | solution.py:469
  164.6 1.9 %copy.9 = bf16[128,2048]{1,0:T(8,128)(2,1)} copy(bf16[128,2048]{1,0:T(8,128)(2,1)} %shard_map.73) | data formatting | bytes 1048576

commit v3 on v2

--- a/solution.py
+++ b/solution.py
@@ -126,8 +126,8 @@
 
 
 MESH = pl.DeviceIdType.MESH
-Z, X, Y, S, FA, FB, R1, R2A, R2B, R3X, R3Y, R4 = 0, 1, 2, 3, 7, 8, 9, 13, 14, 15, 16, 17
-KINDS = 18
+Z, X, Y, S, FA, FB, R1, R2A, R2B, R3X, R3Y, R4, D, RD = 0, 1, 2, 3, 7, 8, 9, 13, 14, 15, 16, 17, 18, 19
+KINDS = 20
 
 
 def flip(value, bit, unit):
@@ -137,7 +137,7 @@
 
 def fused_kernel(
     tokens_ref, gain_ref, w_gate_ref, w_up_ref, w_down_ref, ids_ref, nums_ref, out_ref,
-    rows, sums, from_sibling, diag_in, near_in, z_in, w_in, num_all,
+    rows, sums, from_sibling, diag_in, near_in, z_in, far_in, w_in, num_all,
     send_sem, recv_sem, z_send, num_send, num_recv,
 ):
     grp, loc = lax.axis_index("grp"), lax.axis_index("loc")
@@ -203,6 +203,39 @@
             device_id_type=MESH,
         )
 
+    def copy_d(j, index, target):
+        return pltpu.make_async_remote_copy(
+            src_ref=rows.at[4 * j + 3, own],
+            dst_ref=rows.at[4 * j + 3, own],
+            send_sem=z_send.at[5 + index],
+            recv_sem=recv_sem.at[D * 4 + j],
+            device_id=(grp, target),
+            device_id_type=MESH,
+        )
+
+    def copy_rd(j):
+        return pltpu.make_async_remote_copy(
+            src_ref=sums.at[4 * j + 3],
+            dst_ref=far_in.at[loc],
+            send_sem=send_sem.at[RD * 4 + j],
+            recv_sem=recv_sem.at[RD * 4 + loc],
+            device_id=(grp, j),
+            device_id_type=MESH,
+        )
+
+    def add_far(j):
+        pltpu.make_async_remote_copy(
+            src_ref=far_in.at[j],
+            dst_ref=far_in.at[j],
+            send_sem=send_sem.at[RD * 4 + j],
+            recv_sem=recv_sem.at[RD * 4 + j],
+            device_id=(grp, j),
+            device_id_type=MESH,
+        ).wait_recv()
+        t = 4 * loc + 3
+        total = sums[t].astype(jnp.float32) + far_in[j].astype(jnp.float32)
+        sums[t] = total.astype(jnp.bfloat16)
+
     def copy_x(j):
         return remote(X, j, rows.at[4 * j, own], rows.at[4 * j + 1, own], along_x)
 
@@ -270,13 +303,19 @@
         copy_y(j).start()
         copy_s(j, 0).start()
 
-    def forward(j):
+    def forward(j, diagonal):
         copy_x(j).wait_recv()
-        copy_fa(j).start()
+        if diagonal:
+            copy_fa(j).start()
         copy_s(j, 1).start()
         copy_y(j).wait_recv()
-        copy_fb(j).start()
+        if diagonal:
+            copy_fb(j).start()
         copy_s(j, 2).start()
+
+    def take_diagonal(i):
+        copy_d(plane(i), 2, outer).wait_recv()
+        copy_s(plane(i), 3).start()
 
     def forward_diagonal(j):
         copy_fa(j).wait_recv()
@@ -292,10 +331,12 @@
         sums[t, place, :] = total.astype(jnp.bfloat16)
 
     def reduce_diagonal(j):
+        copy_r2a(j).start()
+        copy_r2b(j).start()
+
+    def add_sibling(j):
         copy_r1(j, 3).wait_recv()
         add(4 * j + 3)
-        copy_r2a(j).start()
-        copy_r2b(j).start()
 
     def reduce_near(j):
         copy_r1(j, 1).wait_recv()
@@ -309,6 +350,14 @@
         add(4 * j + 2, (diag_in.at[j],), first)
         copy_r3y(j).start()
 
+    def reduce_near_only(j):
+        copy_r1(j, 1).wait_recv()
+        add(4 * j + 1)
+        copy_r3x(j).start()
+        copy_r1(j, 2).wait_recv()
+        add(4 * j + 2)
+        copy_r3y(j).start()
+
     def reduce_plane(j):
         copy_r1(j, 0).wait_recv()
         copy_r3x(j).wait_recv()
@@ -344,11 +393,21 @@
 
     w_in[:, :hidden_units] = w_gate_ref[0]
     w_in[:, hidden_units:] = w_up_ref[0]
-    forward(loc)
+    forward(loc, True)
     take_plane(1, far_inner)
     take_plane(2, outer)
     forward_diagonal(loc)
-    forward(plane(1))
+
+    @pl.when(is_inner)
+    def _():
+        copy_d(loc, 0, outer).start()
+        copy_d(loc, 1, far_inner).start()
+
+    @pl.when(mirrored == 0)
+    def _():
+        copy_d(loc, 0, inner).start()
+
+    forward(plane(1), False)
     take_plane(3, outer)
     numerator_copy(
         num_all.at[pl.ds(0, everyone - 1)], num_all.at[pl.ds(0, everyone - 1)], sibling
@@ -383,9 +442,30 @@
         def _():
             @pl.when(k >= 1)
             def _():
-                reduce_diagonal(worked(k - 1))
-
-            @pl.when(k < 3)
+                add_sibling(worked(k - 1))
+
+                @pl.when(k < 3)
+                def _():
+                    copy_rd(worked(k - 1)).start()
+
+                @pl.when(k == 3)
+                def _():
+                    reduce_diagonal(worked(k - 1))
+
+            @pl.when(k == 0)
+            def _():
+                take_diagonal(1)
+
+                @pl.when(is_inner)
+                def _():
+                    take_diagonal(2)
+                    copy_d(plane(2), 2, outer).start()
+
+            @pl.when((k == 1) & (mirrored == 0))
+            def _():
+                take_diagonal(2)
+
+            @pl.when(k == 2)
             def _():
                 forward_diagonal(j)
 
@@ -393,7 +473,11 @@
 
         @pl.when(q == 2)
         def _():
-            @pl.when(k >= 1)
+            @pl.when((k >= 1) & (k < 3))
+            def _():
+                reduce_near_only(worked(k - 1))
+
+            @pl.when(k == 3)
             def _():
                 reduce_near(worked(k - 1))
 
@@ -401,9 +485,13 @@
 
         @pl.when(q == 3)
         def _():
-            @pl.when(k < 2)
-            def _():
-                forward(plane(k + 2))
+            @pl.when(k == 0)
+            def _():
+                forward(plane(2), False)
+
+            @pl.when(k == 1)
+            def _():
+                forward(plane(3), True)
 
             copy_s(j, 3).wait_recv()
 
@@ -425,6 +513,17 @@
             def _():
                 copy_r1(j, which).start()
 
+    add_sibling(loc)
+
+    @pl.when(is_inner)
+    def _():
+        for i in (1, 2, 3):
+            add_far(plane(i))
+
+    @pl.when(mirrored == 0)
+    def _():
+        add_far(plane(1))
+
     reduce_diagonal(loc)
     reduce_plane(worked(2))
     copy_r4(worked(2)).start()
@@ -437,10 +536,18 @@
     out_ref[...] = total.astype(jnp.bfloat16)
 
     copy_z(loc, 0, outer).wait_send()
+    copy_d(loc, 0, outer).wait_send()
+    for i in (1, 2):
+        copy_rd(plane(i)).wait_send()
+    for j in (loc, plane(3)):
+        for make in (copy_fa, copy_fb, copy_r2a, copy_r2b):
+            make(j).wait_send()
 
     @pl.when(is_inner)
     def _():
         copy_z(loc, 1, far_inner).wait_send()
+        copy_d(loc, 1, far_inner).wait_send()
+        copy_d(plane(2), 2, outer).wait_send()
         for i in (1, 2, 3):
             copy_z(plane(i), 1 + i, outer).wait_send()
 
@@ -454,8 +561,8 @@
         for q in range(4):
             copy_s(j, q).wait_send()
             copy_r1(j, q).wait_send()
-        for make in (copy_fa, copy_fb, copy_r2a, copy_r2b, copy_r3x, copy_r3y):
-            make(j).wait_send()
+        copy_r3x(j).wait_send()
+        copy_r3y(j).wait_send()
 
     numerator_copy(
         num_all.at[pl.ds(0, everyone - 1)], num_all.at[pl.ds(0, everyone - 1)], sibling
@@ -478,11 +585,12 @@
             pltpu.VMEM((4, n_rows, width), bf16),
             pltpu.VMEM((4, 2, n_rows, width), bf16),
             pltpu.VMEM((4, n_rows, width), bf16),
+            pltpu.VMEM((4, n_rows, width), bf16),
             pltpu.VMEM((width, 2 * hidden_units), bf16),
             pltpu.VMEM((32, 16, n_rows), bf16),
             pltpu.SemaphoreType.DMA((KINDS * 4,)),
             pltpu.SemaphoreType.DMA((KINDS * 4,)),
-            pltpu.SemaphoreType.DMA((5,)),
+            pltpu.SemaphoreType.DMA((8,)),
             pltpu.SemaphoreType.DMA,
             pltpu.SemaphoreType.DMA,
         ],

time: 167 us -> 158 us (0.946)
  Pallas kernels: 163 us -> 155 us
    pallas_call x1, Pallas kernels: 163 us -> 155 us  [fused(): pl.pallas_call(fused_kernel, out_shape=jax.ShapeDtypeStruct(tokens.shape,...]
where the time goes in v3:
time: 158 us
  Pallas kernels  155 us (98%)
  local copies, waits for them, and re-layouts  3.17 us (2%)
    pallas_call x1, Pallas kernels, fused(): pl.pallas_call(fused_kernel, out_shape=jax.ShapeDtypeStruct(tokens.shape,...  155 us

profile of v3, /device:TPU:0, one launch (start us, length us, event | category | flops | bytes accessed | tf_op | source)
XLA Modules:
  0.0 158.1 jit_solution(13805243235846209321)
XLA Ops:
  0.0 1.3 reshape.3.gain_ref
  1.3 154.9 %shard_map.73 = bf16[128,2048]{1,0:T(8,128)(2,1)} custom-call(bf16[128,2048]{1,0:T(8,128)(2,1)} %tokens_ref.1, bf16[1,2048]{1,0:T(2,128)(2,1)} %reshape.3.gain_ref, bf16[1,2048,384]{2,1,0:T(8,128)(2,1)} %w_gate_ref.1, bf16[1,2048,384]{2,1,0:T(8,128)(2,1)} %w_up_ref.1, bf16[1,384,2048]{2,1,0:T(8,128)(2,1)} %w_down_ref.1, s32[8,128]{1,0:T(8,128)} %bitcast.2, ...), custom_call_target="tpu_custom_call" | custom-call | flops 19327352832 | bytes 4718592 | tf_op jit(solution)/shard_map/pallas_call | solution.py:576
  156.2 1.9 %copy.9 = bf16[128,2048]{1,0:T(8,128)(2,1)} copy(bf16[128,2048]{1,0:T(8,128)(2,1)} %shard_map.73) | data formatting | bytes 1048576

commit v4 on v3

--- a/solution.py
+++ b/solution.py
@@ -137,8 +137,8 @@
 
 def fused_kernel(
     tokens_ref, gain_ref, w_gate_ref, w_up_ref, w_down_ref, ids_ref, nums_ref, out_ref,
-    rows, sums, from_sibling, diag_in, near_in, z_in, far_in, w_in, num_all,
-    send_sem, recv_sem, z_send, num_send, num_recv,
+    rows, sums, from_sibling, diag_in, near_in, z_in, far_in, w_in, w_out, num_all,
+    send_sem, recv_sem, z_send, w_sem, num_send, num_recv,
 ):
     grp, loc = lax.axis_index("grp"), lax.axis_index("loc")
     n_rows, width = tokens_ref.shape
@@ -168,16 +168,18 @@
         other = (me + i) % everyone
         pl.semaphore_signal(barrier, 1, device_id=(other // 4, other % 4), device_id_type=MESH)
 
+    weight_copies = (
+        pltpu.make_async_copy(w_gate_ref.at[0], w_in.at[:, pl.ds(0, hidden_units)], w_sem.at[0]),
+        pltpu.make_async_copy(
+            w_up_ref.at[0], w_in.at[:, pl.ds(hidden_units, hidden_units)], w_sem.at[1]
+        ),
+        pltpu.make_async_copy(w_down_ref.at[0], w_out, w_sem.at[2]),
+    )
     inputs = tokens_ref[...].astype(jnp.float32)
     inv_scale = lax.rsqrt(jnp.mean(inputs * inputs, axis=-1, keepdims=True) + epsilon)
     rows[4 * loc, pl.ds(0, n_rows), :] = (
-        inputs * inv_scale * gain_ref[...].astype(jnp.float32)
+        inputs * inv_scale * gain_ref[...].astype(jnp.float32)[None, :]
     ).astype(jnp.bfloat16)
-    expert_row = lax.broadcasted_iota(jnp.int32, (experts, n_rows), 0)
-    numerators = jnp.zeros((experts, n_rows), jnp.int32)
-    for k in range(ids_ref.shape[0]):
-        numerators += jnp.where(ids_ref[k : k + 1, :] == expert_row, nums_ref[k : k + 1, :], 0)
-    num_all[me] = numerators.astype(jnp.float32).astype(jnp.bfloat16)
     pl.semaphore_wait(barrier, everyone - 1)
 
     def remote(kind, j, source, target, device):
@@ -385,14 +387,19 @@
         copy_z(loc, 0, inner).start()
 
     spread(loc)
+    for copy in weight_copies:
+        copy.start()
+    expert_row = lax.broadcasted_iota(jnp.int32, (experts, n_rows), 0)
+    numerators = jnp.zeros((experts, n_rows), jnp.int32)
+    for k in range(ids_ref.shape[0]):
+        numerators += jnp.where(ids_ref[k : k + 1, :] == expert_row, nums_ref[k : k + 1, :], 0)
+    num_all[me] = numerators.astype(jnp.float32).astype(jnp.bfloat16)
 
     @pl.loop(1, everyone)
     def _(i):
         other = (me + i) % everyone
         numerator_copy(num_all.at[me], num_all.at[me], (other // 4, other % 4)).start()
 
-    w_in[:, :hidden_units] = w_gate_ref[0]
-    w_in[:, hidden_units:] = w_up_ref[0]
     forward(loc, True)
     take_plane(1, far_inner)
     take_plane(2, outer)
@@ -413,6 +420,8 @@
         num_all.at[pl.ds(0, everyone - 1)], num_all.at[pl.ds(0, everyone - 1)], sibling
     ).wait_recv()
 
+    for copy in weight_copies:
+        copy.wait()
     own_expert = grp * 2 + loc // 2
     pick = (expert_row == own_expert).astype(jnp.float32).astype(jnp.bfloat16)
 
@@ -503,7 +512,7 @@
         for part in range(4):
             columns = pl.ds(part * piece, piece)
             result = jnp.dot(
-                hidden, w_down_ref[0, :, columns], preferred_element_type=jnp.float32
+                hidden, w_out[:, columns], preferred_element_type=jnp.float32
             )
             result = (result * weight).astype(jnp.bfloat16)
             sums[t, :, columns] = result[:n_rows]
@@ -576,7 +585,10 @@
     return pl.pallas_call(
         fused_kernel,
         out_shape=jax.ShapeDtypeStruct(tokens.shape, tokens.dtype),
-        in_specs=[pl.BlockSpec(memory_space=pltpu.VMEM)] * 7,
+        in_specs=[
+            pl.BlockSpec(memory_space=pl.ANY if 2 <= operand < 5 else pltpu.VMEM)
+            for operand in range(7)
+        ],
         out_specs=pl.BlockSpec(memory_space=pltpu.VMEM),
         scratch_shapes=[
             pltpu.VMEM((16, 2 * n_rows, width), bf16),
@@ -587,10 +599,12 @@
             pltpu.VMEM((4, n_rows, width), bf16),
             pltpu.VMEM((4, n_rows, width), bf16),
             pltpu.VMEM((width, 2 * hidden_units), bf16),
+            pltpu.VMEM((hidden_units, width), bf16),
             pltpu.VMEM((32, 16, n_rows), bf16),
             pltpu.SemaphoreType.DMA((KINDS * 4,)),
             pltpu.SemaphoreType.DMA((KINDS * 4,)),
             pltpu.SemaphoreType.DMA((8,)),
+            pltpu.SemaphoreType.DMA((3,)),
             pltpu.SemaphoreType.DMA,
             pltpu.SemaphoreType.DMA,
         ],
@@ -602,7 +616,7 @@
             bytes_accessed=2 * width * hidden_units * 3,
             transcendentals=32 * n_rows * hidden_units,
         ),
-    )(tokens, norm_gain.reshape(1, width), w_gate, w_up, w_down, expert_ids.T, gate_num.T)
+    )(tokens, norm_gain, w_gate, w_up, w_down, expert_ids.T, gate_num.T)
 
 
 def shards(tokens, *others):

time: 158 us -> 156 us (0.987)
  Pallas kernels: 155 us -> 153 us
where the time goes in v4:
time: 156 us; the launch traced here: 155 us
  Pallas kernels  153 us (98%)
  local copies, waits for them, and re-layouts  1.88 us (1%)
    pallas_call x1, Pallas kernels, fused(): pl.pallas_call(fused_kernel, out_shape=jax.ShapeDtypeStruct(tokens.shape,...  153 us

profile of v4, /device:TPU:0, one launch (start us, length us, event | category | flops | bytes accessed | tf_op | source)
XLA Modules:
  0.0 155.4 jit_solution(1662065963086729274)
XLA Ops:
  0.0 153.5 %shard_map.73 = bf16[128,2048]{1,0:T(8,128)(2,1)} custom-call(bf16[128,2048]{1,0:T(8,128)(2,1)} %tokens_ref.1, bf16[2048]{0:T(1024)(128)(2,1)} %gain_ref.1, bf16[1,2048,384]{2,1,0:T(8,128)(2,1)} %w_gate_ref.1, bf16[1,2048,384]{2,1,0:T(8,128)(2,1)} %w_up_ref.1, bf16[1,384,2048]{2,1,0:T(8,128)(2,1)} %w_down_ref.1, s32[8,128]{1,0:T(8,128)} %bitcast.2, ...), custom_call_target="tpu_custom_call" | custom-call | flops 19327352832 | bytes 4718592 | tf_op jit(solution)/shard_map/pallas_call | solution.py:585
  153.5 1.9 %copy.9 = bf16[128,2048]{1,0:T(8,128)(2,1)} copy(bf16[128,2048]{1,0:T(8,128)(2,1)} %shard_map.73) | data formatting | bytes 1048576
